TPU v7x, 512 devices: a whole 4x8x8 slice. The times are simulated.
512 devices in a mesh: section: 32 (over x_hi, z, core), rep: 16 (over y, x_lo).
Axes of the slice: x: 4 (x_hi: 2, x_lo: 2; x = x_hi * 2 + x_lo), y: 8, z: 8, core: 2. Of those that a mesh axis runs over, the one named last changes fastest.
Arguments:
- features: bfloat16 [65536, 256], P(('section', 'rep')), may hold values from -6 to 6
- weight: bfloat16 [256, 256], replicated, may hold values from -0.375 to 0.375
- cotangent: bfloat16 [65536, 256], P(('section', 'rep')), may hold values from -6 to 6
- tile_values: bfloat16 [32, 16, 32, 2, 128, 128], P('section', 'rep'), may hold values from -0.09375 to 0.09375
- tile_cols: int32 [32, 16, 32, 2], P('section', 'rep'), may hold values from 0 to 15
- tile_counts: int32 [32, 16, 32], P('section', 'rep'), may hold values from 0 to 2, as said below
Outputs:
- output: bfloat16 [65536, 256], P(('section', 'rep'))
- grad_features: bfloat16 [65536, 256], P(('section', 'rep'))
- grad_weight: float32 [256, 256], replicated
Inputs may be any that keep to these rules, and one draw needn't show every extreme that they name: `tile_cols`: column tile of each slot inside the column section's block of 16 tiles; slots at or past the count are unused. `tile_counts`: live slots of each list; every row block has one column section whose list holds 2 live tiles.
All inputs are finite; a program needn't handle non-finite values.
Results may differ from a plain program's by a relative error of at most 0.023.
Values may be sent and summed in bfloat16 or wider, within the bound.
A program may use at most 64 MiB of HBM per device.

v0:
```python
import math

import jax
import jax.numpy as jnp
from jax import lax
from jax.sharding import PartitionSpec as P


def body(features, weight, cotangent, tile_values, tile_cols, tile_counts):
    sections = lax.axis_size("section")
    groups = lax.axis_size("rep")
    tile = features.shape[0]
    width = features.shape[1]
    slots = tile_values.shape[3]
    moved_tiles, moved_cols, moved_counts = (
        lax.all_to_all(tile_values, "section", split_axis=2, concat_axis=0, tiled=True),
        lax.all_to_all(tile_cols, "section", split_axis=2, concat_axis=0, tiled=True),
        lax.all_to_all(tile_counts, "section", split_axis=2, concat_axis=0, tiled=True),
    )
    moved_tiles = moved_tiles.reshape(sections, slots, tile, tile)
    moved_cols = moved_cols.reshape(sections, slots)
    moved_live = jnp.arange(slots)[None, :] < moved_counts.reshape(sections)[:, None]
    moved_masked = jnp.where(moved_live[:, :, None, None], moved_tiles, jnp.zeros_like(moved_tiles))
    section_block = lax.all_gather(features, "rep", axis=0, tiled=True).reshape(groups, tile, width)
    chosen = section_block[moved_cols]
    partials = jnp.einsum(
        "tskj,tsjd->tkd", moved_masked, chosen, preferred_element_type=jnp.float32
    )
    returned = lax.all_to_all(partials, "section", split_axis=0, concat_axis=0, tiled=True)
    summed = jnp.sum(returned, axis=0)
    aggregated = summed.astype(jnp.bfloat16)
    pre = jnp.dot(aggregated, weight, preferred_element_type=jnp.float32)
    output = jax.nn.silu(pre).astype(jnp.bfloat16)
    sig = jax.nn.sigmoid(pre)
    grad_pre = (cotangent.astype(jnp.float32) * sig * (1.0 + pre * (1.0 - sig))).astype(
        jnp.bfloat16
    )
    local_terms = jnp.dot(aggregated.T, grad_pre, preferred_element_type=jnp.float32)
    total_nodes = tile * sections * groups
    grad_weight = lax.psum(local_terms, ("section", "rep")) / math.sqrt(total_nodes)
    grad_aggr = jnp.dot(grad_pre, weight.T, preferred_element_type=jnp.float32).astype(jnp.bfloat16)
    row_grads = lax.all_gather(grad_aggr, "section", axis=0, tiled=True).reshape(
        sections, tile, width
    )
    contrib = jnp.einsum(
        "tskj,tkd->tsjd", moved_masked, row_grads, preferred_element_type=jnp.float32
    )
    first = jnp.int32(0) // tile
    number = tile * lax.axis_size("rep") // tile
    picks = (moved_cols[:, :, None] - first == jnp.arange(number)[None, None, :]).astype(
        jnp.float32
    )
    terms = jnp.einsum("tsq,tsjd->qjd", picks, contrib)
    grad_features = lax.psum_scatter(
        terms.reshape(tile * lax.axis_size("rep"), width).astype(jnp.bfloat16),
        "rep",
        scatter_dimension=0,
        tiled=True,
    )
    return (output, grad_features, grad_weight)


def solution(mesh):
    return jax.shard_map(
        body,
        mesh=mesh,
        in_specs=(
            P(("section", "rep"), None),
            P(),
            P(("section", "rep"), None),
            P("section", "rep", None, None, None, None),
            P("section", "rep", None, None),
            P("section", "rep", None),
        ),
        out_specs=(P(("section", "rep"), None), P(("section", "rep"), None), P()),
        check_vma=False,
    )
```

profile of v0, /device:TPU:1, one launch (start us, length us, event | category | flops | bytes accessed | tf_op | source)
XLA Modules:
  0.0 669.0 jit_solution(5240054267309424484)
XLA Ops:
  7.2 1.4 copy.21
  8.6 14.4 %all-to-all-start = ((s32[1,1,32]{1,0,2:T(1,128)}), s32[1,1,32]{1,0,2:T(1,128)S(1)}, u32[]{:S(2)}, u32[]{:S(2)}) async-start(s32[1,1,32]{1,0,2:T(1,128)} %copy.21), calls=%async_computation | async-start | bytes 32768 | tf_op jit(solution)/shard_map/all_to_all | solution.py:18
  23.0 0.8 copy.23
  23.8 8.5 %all-to-all-done = s32[1,1,32]{1,0,2:T(1,128)S(1)} async-done(((s32[1,1,32]{1,0,2:T(1,128)}), s32[1,1,32]{1,0,2:T(1,128)S(1)}, u32[]{:S(2)}, u32[]{:S(2)}) %all-to-all-start) | async-done | bytes 160 | tf_op jit(solution)/shard_map/all_to_all | solution.py:18
  32.3 12.8 %all_to_all.32 = s32[1,1,32,2]{3,1,0,2:T(1,128)S(1)} all-to-all(s32[1,1,32,2]{3,1,0,2:T(1,128)S(1)} %copy.23), channel_id=1, replica_groups=mesh['section'=32,'rep'=16] {'section'}, dimensions={2} | all-to-all | bytes 512 | tf_op jit(solution)/shard_map/all_to_all | solution.py:17
  45.1 4.5 all-to-all-start.1
  49.6 0.0 all-gather.3.cloned.1.call-start
  49.6 0.7 all-gather.3.cloned.1.call-update
  50.3 0.0 all-gather.5.cloned.1.call-start
  50.4 0.7 reduce
  51.0 0.1 iota_compare_fusion.1
  51.1 0.1 copy.24
  51.2 0.1 copy.25
  51.3 0.1 reshape.96
  51.4 67.7 %all-gather.3.cloned.1.call-done = bf16[2048,256]{1,0:T(8,128)(2,1)} async-done(((bf16[128,256]{1,0:T(8,128)(2,1)}), bf16[2048,256]{1,0:T(8,128)(2,1)}) %all-gather.3.cloned.1.call-update) | async-done | bytes 1048592 | tf_op jit(solution)/shard_map/all_gather | solution.py:24
  119.1 4.0 gather_fusion
  123.1 2.9 convolution_bitcast_fusion
  126.0 118.0 %all_to_all.33 = f32[32,128,256]{2,1,0:T(8,128)} all-to-all(f32[32,128,256]{2,1,0:T(8,128)S(1)} %convolution_bitcast_fusion), channel_id=1, replica_groups=mesh['section'=32,'rep'=16] {'section'}, dimensions={0} | all-to-all | bytes 8388608 | tf_op jit(solution)/shard_map/all_to_all | solution.py:29
  244.0 2.5 reduce_sum.9
  246.5 0.8 multiply_convert_fusion.1
  247.3 0.8 convolution_convert_fusion
  248.1 0.0 all-gather.5.cloned.1.call-update
  248.2 0.0 all-reduce.2.cloned.1.call-start
  248.2 0.9 fusion.7
  249.2 0.0 reduce-scatter.2.cloned.1.call-start
  249.2 81.6 %all-gather.5.cloned.1.call-done = bf16[4096,256]{1,0:T(8,128)(2,1)} async-done(((bf16[128,256]{1,0:T(8,128)(2,1)}), bf16[4096,256]{1,0:T(8,128)(2,1)}) %all-gather.5.cloned.1.call-update) | async-done | bytes 2097168 | tf_op jit(solution)/shard_map/all_gather | solution.py:42
  330.8 3.5 fusion.2
  334.3 2.4 bitcast_convert_fusion
  336.7 1.3 copy.29
  338.0 261.7 %all-reduce.2.cloned.1.call-done = f32[256,256]{1,0:T(8,128)} async-done(((f32[256,256]{1,0:T(8,128)}), f32[256,256]{1,0:T(8,128)}) %all-reduce.2.cloned.1.call-update) | async-done | bytes 262160 | tf_op jit(solution)/shard_map/psum | solution.py:40
  599.7 1.7 broadcast_multiply_fusion
  601.3 61.1 %reduce-scatter.2.cloned.1.call-done = bf16[128,256]{1,0:T(8,128)(2,1)} async-done(((bf16[2048,256]{1,0:T(8,128)(2,1)}), bf16[128,256]{1,0:T(8,128)(2,1)}) %reduce-scatter.2.cloned.1.call-update) | async-done | bytes 65552 | tf_op jit(solution)/shard_map/reduce_scatter | solution.py:54
  (9 shorter events, 0.1 us)
Async XLA Ops:
  7.2 239.3 %copy-start = (bf16[256,256]{1,0:T(8,128)(2,1)S(1)}, bf16[256,256]{1,0:T(8,128)(2,1)}, u32[]{:S(2)}) copy-start(bf16[256,256]{1,0:T(8,128)(2,1)} %param.7) | copy-start | bytes 393220
  8.6 23.7 %all-to-all-start = ((s32[1,1,32]{1,0,2:T(1,128)}), s32[1,1,32]{1,0,2:T(1,128)S(1)}, u32[]{:S(2)}, u32[]{:S(2)}) async-start(s32[1,1,32]{1,0,2:T(1,128)} %copy.21), calls=%async_computation | async-start | bytes 32768 | tf_op jit(solution)/shard_map/all_to_all | solution.py:18
  45.1 78.0 %all-to-all-start.1 = ((bf16[1,1,32,2,128,128]{5,4,3,1,0,2:T(8,128)(2,1)}), bf16[1,1,32,2,128,128]{5,4,3,1,0,2:T(8,128)(2,1)S(1)}, u32[]{:S(2)}, u32[]{:S(2)}) async-start(bf16[1,1,32,2,128,128]{5,4,3,1,0,2:T(8,128)(2,1)} %bitcast.36), calls=%async_computation.1 | async-start | bytes 4194304 | tf_op jit(solution)/shard_map/all_to_all | solution.py:16
  49.6 69.5 %all-gather.3.cloned.1.call-start = ((), (), s32[]{:S(2)}) async-start(), calls=%async_computation.5 | async-start | bytes 1114112 | tf_op jit(solution)/shard_map/all_gather | solution.py:24
  50.3 280.5 %all-gather.5.cloned.1.call-start = ((), (), s32[]{:S(2)}) async-start(), calls=%async_computation.6 | async-start | bytes 2162688 | tf_op jit(solution)/shard_map/all_gather | solution.py:42
  244.0 3.3 copy-start.1
  248.2 351.5 %all-reduce.2.cloned.1.call-start = ((), (), s32[]{:S(2)}) async-start(), calls=%async_computation.8 | async-start | bytes 524288 | tf_op jit(solution)/shard_map/psum | solution.py:40
  249.2 413.3 %reduce-scatter.2.cloned.1.call-start = ((), (), s32[]{:S(2)}) async-start(), calls=%async_computation.7 | async-start | bytes 1114112 | tf_op jit(solution)/shard_map/reduce_scatter | solution.py:54
Sparse Core Ops, SparseCore 0:
  52.5 66.5 all-gather.2
  248.3 82.4 all-gather.4
  336.4 263.2 all-reduce.1
  603.1 59.2 reduce-scatter.1
where the time goes:
time: 679 us; the launch traced here: 669 us
  waiting for transfers between devices  481 us (71%)
  blocking collectives  131 us (19%)
  starting transfers between devices  19.1 us (3%)
  between operations  13.8 us (2%)
  matrix products  11.4 us (2%)
  local copies, waits for them, and re-layouts  7.73 us (1%)
    psum x1, waiting for transfers between devices, body(): lax.psum(local_terms, ('section', 'rep')) / math.sqrt(total_nodes)  262 us
    all_to_all x1, blocking collectives, body(): lax.all_to_all(partials, 'section', split_axis=0, concat_axis=0, tiled=True)  118 us
    all_gather x1, waiting for transfers between devices, body(): lax.all_gather(grad_aggr, 'section', axis=0, tiled=True)  81.6 us
    all_gather x1, waiting for transfers between devices, body(): lax.all_gather(features, 'rep', axis=0, tiled=True)  67.7 us
    reduce_scatter x1, waiting for transfers between devices, body(): lax.psum_scatter(terms.reshape(tile * lax.axis_size('rep'), width).astype...  61.1 us
    all_to_all x1, starting transfers between devices, body(): lax.all_to_all(tile_counts, 'section', split_axis=2, concat_axis=0, tiled...  14.4 us
  transfers between devices with their start and end apart: 6, of which 5 were waited for; matrix products, arithmetic and copies ran while one was open for 2% of the time, Pallas kernels for 0%

commit v1 on v0

v1 whole, which is shorter than its diff:
```python
import jax
import jax.numpy as jnp
from jax import lax
from jax.experimental import pallas as pl
from jax.experimental.pallas import tpu as pltpu
from jax.sharding import PartitionSpec as P

MESH = pl.DeviceIdType.MESH
F32 = jnp.float32
BF16 = jnp.bfloat16
NX, NY, NZ = 4, 8, 8
ZH = NZ // 2
GROUP = 8
SLOTS = 2
TILE = 128
D = 256
TERMS = ZH * GROUP * SLOTS
ZERO = TERMS


def device(x, y, z, k):
    return ((x // 2) * (2 * NZ) + z * 2 + k, y * 2 + x % 2)


def kernel(
    feat_ref, weight_ref, cot_ref, cols_ref, counts_ref, tiles_ref,
    out_ref, gf_ref, gw_ref,
    tiles_rx, meta_tx, meta_rx, meta_sm, prev_sm, last_sm,
    feats, part_tx, part_rx, grad_tx, grad_rx, chain,
    sib_tx, sib_rx, up_tx, up_rx, down_tx, down_rx, own_tx, own_rx,
    gw1_tx, gw1_rx, gw2_tx, gw2_rx, gw3_rx, gw4_rx, gw5_rx,
    local_sem, tile_s, tile_r, meta_s, meta_r, gat_s, gat_r,
    up_s, up_r, down_s, down_r, agd_s, agd_r, part_s, part_r, grad_s, grad_r,
    sib_s, sib_r, ups_s, ups_r, downs_s, downs_r, own_s, own_r,
    gw_s, gw_r,
):
    section, rep = lax.axis_index("section"), lax.axis_index("rep")
    xh, z, k = section // (2 * NZ), (section // 2) % NZ, section % 2
    y, xl = rep // 2, rep % 2
    x = 2 * xh + xl
    yh, yp, zh, zp = y // 2, y % 2, z // 2, z % 2
    member = x * 2 + k
    turn = 1 - 2 * k
    xpair = (x + turn * (1 - 2 * xl) + NX) % NX
    ypair = (y + turn * (1 - 2 * yp) + NY) % NY
    zpair = (z + turn * (1 - 2 * zp) + NZ) % NZ
    mine = xl * 4 + yp * 2 + zp
    sibling = device(x, y, z, 1 - k)
    alone = jnp.logical_and(xl == k, xh == yp)
    away = jnp.logical_not(alone)

    def swap(core, a, b):
        return a + core * (b - a), b - core * (b - a)

    u0, v0 = swap(k, yh, zh)
    uh, vh = swap(xl, yh, zh)
    vs = [(v0 + i) % ZH for i in range(ZH)]

    def gatherer(i, a):
        yy, zz = swap(xl, uh, (vh + i) % ZH)
        return device(2 * ((xh + a) % 2) + k, 2 * yy + xh, 2 * zz + zp, xl)

    def owner(i, e):
        yy, zz = swap(k, u0, vs[i])
        return device(2 * yp + k, 2 * yy + (yp + e) % 2, 2 * zz + zp, xl)

    def along(j):
        yy, zz = swap(k, (u0 + j + ZH) % ZH, v0)
        return device(x, 2 * yy + yp, 2 * zz + zp, k)

    def group(o):
        px, py, pz = (xl + o // 4) % 2, (yp + (o // 2) % 2) % 2, (zp + o % 2) % 2
        return px, py, pz, px * 4 + py * 2 + pz

    def peer(o):
        px, py, pz, p = group(o)
        dev = device(xpair if o & 4 else x, ypair if o & 2 else y, zpair if o & 1 else z, k)
        return (py, pz, px), p, dev

    def copy(src, dst, send, recv, dev):
        return pltpu.make_async_remote_copy(
            src_ref=src, dst_ref=dst, send_sem=send, recv_sem=recv,
            device_id=dev, device_id_type=MESH,
        )

    sent = []

    def send(src, dst, ssem, rsem, dev):
        c = copy(src, dst, ssem, rsem, dev)
        c.start()
        sent.append(c)

    def arrived(dst, ssem, rsem):
        copy(dst, dst, ssem, rsem, sibling).wait_recv()

    ypeers = [(y + i) % NY for i in range(1, NY)]
    zpeers = [(z + i) % NZ for i in range(1, NZ)]
    mpeers = [(member + i) % GROUP for i in range(1, GROUP)]

    own_tiles = pltpu.make_async_copy(
        tiles_ref.at[yp, :, zp, xl], tiles_rx.at[mine], local_sem.at[0]
    )
    own_tiles.start()

    barrier = pltpu.get_barrier_semaphore()
    everyone = (
        [device(x, j, z, k) for j in ypeers]
        + [device(x, y, j, k) for j in zpeers]
        + [device(j // 2, y, z, j % 2) for j in mpeers]
        + [peer(o)[2] for o in (3, 5, 6, 7)]
        + [f(i, a) for f in (gatherer, owner) for i in range(ZH) for a in range(2) if i or a]
    )
    for dev in everyone:
        pl.semaphore_signal(barrier, inc=1, device_id=dev, device_id_type=MESH)

    @pl.when(away)
    def _():
        for dev in (gatherer(0, 0), owner(0, 0)):
            pl.semaphore_signal(barrier, inc=1, device_id=dev, device_id_type=MESH)

    pl.semaphore_wait(barrier, len(everyone) + jnp.where(away, 2, 0))

    own_slot = feats.at[xl, uh, vh, yp]

    @pl.when(alone)
    def _():
        feats[xl, uh, vh, yp] = feat_ref[...]

    @pl.when(away)
    def _():
        copy(feat_ref, own_slot, gat_s.at[0, 0], gat_r.at[vh, yp], gatherer(0, 0)).start()

    for i in range(ZH):
        for a in range(2):
            if i or a:
                send(feat_ref, own_slot, gat_s.at[i, a], gat_r.at[vh, yp], gatherer(i, a))

    dead = lax.broadcasted_iota(jnp.int32, (SLOTS, 32), 0) >= counts_ref[...]
    meta_tx[...] = jnp.zeros_like(meta_tx)
    meta_tx[0:SLOTS, 0:32] = cols_ref[...] + jnp.where(dead, 2 * NY, 0)
    for o in range(1, GROUP):
        which, p, dev = peer(o)
        send(meta_tx, meta_rx.at[mine], meta_s.at[o], meta_r.at[mine], dev)
    for o in range(1, GROUP):
        (ch, cz, ck), p, dev = peer(o)
        send(tiles_ref.at[ch, :, cz, ck], tiles_rx.at[mine], tile_s.at[o], tile_r.at[mine], dev)
    meta_rx[mine] = meta_tx[...]

    up, down = along(1), along(-1)

    def uu(j):
        return (u0 + j + ZH) % ZH

    def gather_up(s, i):
        part = feats.at[k, uu(-s), vs[i]]
        send(part, part, up_s.at[s, i], up_r.at[s, i], up)

    def gather_down(s, i):
        part = feats.at[k, uu(s), vs[i]]
        send(part, part, down_s.at[s, i], down_r.at[s, i], down)

    def gather_sibling(j):
        part = feats.at[k, uu(j)]
        send(part, part, agd_s.at[j], agd_r.at[uu(j)], sibling)

    for i in range(ZH):
        arrived(feats.at[k, u0, vs[i], 1 - yp], gat_s.at[i, 1], gat_r.at[vs[i], 1 - yp])
        if i == 0:
            @pl.when(away)
            def _():
                arrived(feats.at[k, u0, v0, yp], gat_s.at[0, 0], gat_r.at[v0, yp])
        else:
            arrived(feats.at[k, u0, vs[i], yp], gat_s.at[i, 0], gat_r.at[vs[i], yp])
        gather_up(0, i)
        gather_down(0, i)
    gather_sibling(0)
    for i in (0, 2, 1, 3):
        arrived(feats.at[k, uu(-1), vs[i]], up_s.at[0, i], up_r.at[0, i])
        if i < 2:
            gather_up(1, i)
        arrived(feats.at[k, uu(1), vs[i]], down_s.at[0, i], down_r.at[0, i])
        if i >= 2:
            gather_down(1, i)
    gather_sibling(1)
    gather_sibling(3)
    for i in (0, 1):
        arrived(feats.at[k, uu(2), vs[i]], up_s.at[1, i], up_r.at[1, i])
        arrived(feats.at[k, uu(2), vs[i + 2]], down_s.at[1, i + 2], down_r.at[1, i + 2])
    gather_sibling(2)

    for o in range(1, GROUP):
        p = peer(o)[1]
        arrived(meta_rx.at[p], meta_s.at[o], meta_r.at[p])
    to_scalar = pltpu.make_async_copy(meta_rx, meta_sm, local_sem.at[1])
    to_scalar.start()
    to_scalar.wait()

    def column_section(c):
        return yp * (2 * NZ) + c * 4 + zp * 2 + xl

    @pl.loop(0, ZH * 2 * NY)
    def _(q):
        last_sm[q] = ZERO

    @pl.loop(0, TERMS)
    def _(i):
        c, o, s = i // (GROUP * SLOTS), (i // SLOTS) % GROUP, i % SLOTS
        col = meta_sm[group(o)[3], s, column_section(c)] % (2 * NY)
        prev_sm[i] = last_sm[c * 2 * NY + col]
        for q in range(2 * NY):
            last_sm[c * 2 * NY + q] = jnp.where(col == q, i, last_sm[c * 2 * NY + q])

    chain[ZERO] = jnp.zeros((D, TILE), F32)

    for c in range(ZH):
        arrived(feats.at[1 - k, c], agd_s.at[c], agd_r.at[c])

    def live_tiles(p, c):
        tiles, codes = [], []
        for s in range(SLOTS):
            code = meta_sm[p, s, column_section(c)]
            tile = tiles_rx[p, c, s]
            tiles.append(jnp.where(code < 2 * NY, tile, jnp.zeros_like(tile)))
            codes.append(code % (2 * NY))
        return jnp.concatenate(tiles, axis=1), codes

    total = None
    for o in (1, 2, 4, 3, 5, 6, 7, 0):
        which, p, dev = peer(o)
        if o == 0:
            own_tiles.wait()
        else:
            arrived(tiles_rx.at[p], tile_s.at[o], tile_r.at[p])
        acc = jnp.zeros((TILE, D), F32)
        for c in range(ZH):
            pair, cols = live_tiles(p, c)
            rows = []
            for col in cols:
                u, v = swap(col % 2, col // 4, c)
                rows.append(feats[col % 2, u, v, (col // 2) % 2])
            rows = jnp.concatenate(rows, axis=0)
            acc += jnp.dot(pair, rows, preferred_element_type=F32)
        if o == 0:
            total = acc
        else:
            part_tx[o] = acc.astype(BF16)
            send(part_tx.at[o], part_rx.at[mine], part_s.at[o], part_r.at[mine], dev)
    for o in range(1, GROUP):
        p = peer(o)[1]
        arrived(part_rx.at[p], part_s.at[o], part_r.at[p])
        total += part_rx[p].astype(F32)

    aggregated = total.astype(BF16)
    weight = weight_ref[...]
    pre = jnp.dot(aggregated, weight, preferred_element_type=F32)
    sig = lax.logistic(pre)
    out_ref[...] = (pre * sig).astype(BF16)
    grad_pre = (cot_ref[...].astype(F32) * sig * (1.0 + pre * (1.0 - sig))).astype(BF16)
    grad_tx[...] = lax.dot_general(
        weight, grad_pre, (((1,), (1,)), ((), ())), preferred_element_type=F32
    ).astype(BF16)
    for o in range(1, GROUP):
        which, p, dev = peer(o)
        send(grad_tx, grad_rx.at[mine], grad_s.at[o], grad_r.at[mine], dev)

    terms = lax.dot_general(
        aggregated, grad_pre, (((0,), (0,)), ((), ())), preferred_element_type=F32
    )
    for i in range(NZ):
        for j in range(GROUP):
            r0, c0 = i * 32 + (j % 4) * 8, (j // 4) * 128
            gw1_tx[i, j] = terms[r0:r0 + 8, c0:c0 + 128]
    for i, j in enumerate(zpeers):
        send(gw1_tx.at[j], gw1_rx.at[z], gw_s.at[0, i], gw_r.at[0, z], device(x, y, j, k))
    gw1_rx[z] = gw1_tx[z]

    for o in range(GROUP):
        which, p, dev = peer(o)
        if o == 0:
            grads = grad_tx[...]
        else:
            arrived(grad_rx.at[p], grad_s.at[o], grad_r.at[p])
            grads = grad_rx[p]
        for c in range(ZH):
            pair, cols = live_tiles(p, c)
            both = jnp.dot(grads, pair, preferred_element_type=F32)
            for s in range(SLOTS):
                i = c * GROUP * SLOTS + o * SLOTS + s
                chain[i] = both[:, s * TILE:(s + 1) * TILE] + chain[prev_sm[i]]

    for i, j in enumerate(zpeers):
        arrived(gw1_rx.at[j], gw_s.at[0, i], gw_r.at[0, j])
    gw2_tx[...] = jnp.sum(gw1_rx[...], axis=0)
    for i, j in enumerate(mpeers):
        send(gw2_tx.at[j], gw2_rx.at[member], gw_s.at[1, i], gw_r.at[1, member], device(j // 2, y, z, j % 2))
    gw2_rx[member] = gw2_tx[member]

    def block(half, u, v, e):
        yy, c = swap(half, u, v)
        return chain[last_sm[c * 2 * NY + (2 * yy + e) * 2 + half]]

    for j in (2, 1, 3, 0):
        u = (v0 + j) % ZH
        for v in range(ZH):
            for e in range(2):
                sib_tx[u, v, e] = block(1 - k, u, v, e).astype(BF16)
        send(sib_tx.at[u], sib_rx.at[u], sib_s.at[j], sib_r.at[u], sibling)

    for i, j in enumerate(mpeers):
        arrived(gw2_rx.at[j], gw_s.at[1, i], gw_r.at[1, j])
    gw3_rx[y] = jnp.sum(gw2_rx[...], axis=0)
    for i, j in enumerate(ypeers):
        send(gw3_rx.at[y], gw3_rx.at[y], gw_s.at[2, i], gw_r.at[2, y], device(x, j, z, k))

    def both_cores(u, v, e):
        return block(k, u, v, e) + sib_rx[u, v, e].astype(F32)

    def sibling_arrived(u):
        arrived(sib_rx.at[u], sib_s.at[0], sib_r.at[u])

    def reduce_step(u, i, slot, before, tx, rx, ssem, rsem, dev):
        if before is not None:
            arrived(rx.at[before], ssem.at[before], rsem.at[before])
        for e in range(2):
            value = both_cores(u, vs[i], e)
            if before is not None:
                value += rx[before, e].astype(F32)
            tx[slot, e] = value.astype(BF16)
        send(tx.at[slot], rx.at[slot], ssem.at[slot], rsem.at[slot], dev)

    ups = (up_tx, up_rx, ups_s, ups_r, up)
    downs = (down_tx, down_rx, downs_s, downs_r, down)
    sibling_arrived(uu(2))
    for i in range(2):
        reduce_step(uu(2), i, i, None, *ups)
        reduce_step(uu(2), i + 2, i, None, *downs)
    sibling_arrived(uu(1))
    sibling_arrived(uu(-1))
    for i in range(2):
        reduce_step(uu(1), i + 2, i + 4, None, *ups)
        reduce_step(uu(-1), i, i + 2, None, *downs)

    for i, j in enumerate(ypeers):
        arrived(gw3_rx.at[j], gw_s.at[2, i], gw_r.at[2, j])
    gw4_rx[member] = jnp.sum(gw3_rx[...], axis=0)
    for i, j in enumerate(mpeers):
        send(gw4_rx.at[member], gw4_rx.at[member], gw_s.at[3, i], gw_r.at[3, member], device(j // 2, y, z, j % 2))

    for i in range(2):
        reduce_step(uu(1), i, i + 2, i, *ups)
        reduce_step(uu(-1), i + 2, i + 4, i, *downs)

    for i, j in enumerate(mpeers):
        arrived(gw4_rx.at[j], gw_s.at[3, i], gw_r.at[3, j])
    gw5_rx[z] = gw4_rx[...]
    for i, j in enumerate(zpeers):
        send(gw5_rx.at[z], gw5_rx.at[z], gw_s.at[4, i], gw_r.at[4, z], device(x, y, j, k))

    sibling_arrived(u0)
    for i in (2, 3, 1, 0):
        arrived(up_rx.at[i + 2], ups_s.at[i + 2], ups_r.at[i + 2])
        arrived(down_rx.at[i + 2], downs_s.at[i + 2], downs_r.at[i + 2])
        for a in (1, 0):
            e = (yp + a) % 2
            value = both_cores(u0, vs[i], e) + up_rx[i + 2, e].astype(F32) + down_rx[i + 2, e].astype(F32)
            own_tx[i, a] = value.astype(BF16)
            if i or a:
                send(own_tx.at[i, a], own_rx.at[v0, xh], own_s.at[i, a], own_r.at[v0, xh], owner(i, a))

    @pl.when(alone)
    def _():
        own_rx[v0, xh] = own_tx[0, 0]

    @pl.when(away)
    def _():
        copy(own_tx.at[0, 0], own_rx.at[v0, xh], own_s.at[0, 0], own_r.at[v0, xh], owner(0, 0)).start()

    for i, j in enumerate(zpeers):
        arrived(gw5_rx.at[j], gw_s.at[4, i], gw_r.at[4, j])
    scale = 1.0 / 256.0
    for i in range(NZ):
        for j in range(GROUP):
            r0, c0 = i * 32 + (j % 4) * 8, (j // 4) * 128
            gw_ref[r0:r0 + 8, c0:c0 + 128] = gw5_rx[i, j] * scale

    for i in range(ZH):
        for a in range(2):
            v, h = (vh + i) % ZH, (xh + a) % 2
            if i or a:
                arrived(own_rx.at[v, h], own_s.at[i, a], own_r.at[v, h])

    @pl.when(away)
    def _():
        arrived(own_rx.at[vh, xh], own_s.at[0, 0], own_r.at[vh, xh])

    gf_ref[...] = jnp.sum(own_rx[...].astype(F32), axis=(0, 1)).T.astype(BF16)

    @pl.when(away)
    def _():
        copy(own_tx.at[0, 0], own_rx.at[v0, xh], own_s.at[0, 0], own_r.at[v0, xh], owner(0, 0)).wait_send()
        copy(feat_ref, own_slot, gat_s.at[0, 0], gat_r.at[vh, yp], gatherer(0, 0)).wait_send()

    for c in sent:
        c.wait_send()


def finish(out_in, gf_in, gw_in, out_ref, gf_ref, gw_ref):
    out_ref[...] = out_in[...]
    gf_ref[...] = gf_in[...]
    gw_ref[...] = gw_in[...]


def body(features, weight, cotangent, tile_values, tile_cols, tile_counts):
    cols = tile_cols.reshape(32, SLOTS).T
    counts = tile_counts.reshape(1, 32)
    tiles = tile_values.reshape(2, ZH, 2, 2, SLOTS, TILE, TILE)
    dma, vmem = pltpu.SemaphoreType.DMA, pltpu.VMEM
    spec = pl.BlockSpec(memory_space=pltpu.VMEM)
    block = (D, TILE)
    results = pl.pallas_call(
        kernel,
        out_shape=(
            jax.ShapeDtypeStruct((TILE, D), BF16),
            jax.ShapeDtypeStruct((TILE, D), BF16),
            jax.ShapeDtypeStruct((D, D), F32),
        ),
        in_specs=[spec] * 5 + [pl.BlockSpec(memory_space=pl.ANY)],
        out_specs=(spec,) * 3,
        scratch_shapes=[
            vmem((GROUP, ZH, SLOTS, TILE, TILE), BF16),
            vmem((8, 128), jnp.int32),
            vmem((GROUP, 8, 128), jnp.int32),
            pltpu.SMEM((GROUP, 8, 128), jnp.int32),
            pltpu.SMEM((TERMS,), jnp.int32),
            pltpu.SMEM((ZH * 2 * NY,), jnp.int32),
            vmem((2, ZH, ZH, 2, TILE, D), BF16),
            vmem((GROUP, TILE, D), BF16),
            vmem((GROUP, TILE, D), BF16),
            vmem(block, BF16),
            vmem((GROUP,) + block, BF16),
            vmem((TERMS + 1,) + block, F32),
            vmem((ZH, ZH, 2) + block, BF16),
            vmem((ZH, ZH, 2) + block, BF16),
            vmem((6, 2) + block, BF16),
            vmem((6, 2) + block, BF16),
            vmem((6, 2) + block, BF16),
            vmem((6, 2) + block, BF16),
            vmem((ZH, 2) + block, BF16),
            vmem((ZH, 2) + block, BF16),
            vmem((NZ, GROUP, 8, 128), F32),
            vmem((NZ, GROUP, 8, 128), F32),
            vmem((GROUP, 8, 128), F32),
            vmem((GROUP, 8, 128), F32),
            vmem((NY, 8, 128), F32),
            vmem((GROUP, 8, 128), F32),
            vmem((NZ, GROUP, 8, 128), F32),
            dma((2,)),
            dma((GROUP,)), dma((GROUP,)),
            dma((GROUP,)), dma((GROUP,)),
            dma((ZH, 2)), dma((ZH, 2)),
            dma((2, ZH)), dma((2, ZH)),
            dma((2, ZH)), dma((2, ZH)),
            dma((ZH,)), dma((ZH,)),
            dma((GROUP,)), dma((GROUP,)),
            dma((GROUP,)), dma((GROUP,)),
            dma((ZH,)), dma((ZH,)),
            dma((6,)), dma((6,)),
            dma((6,)), dma((6,)),
            dma((ZH, 2)), dma((ZH, 2)),
            dma((5, 8)), dma((5, 8)),
        ],
        compiler_params=pltpu.CompilerParams(
            collective_id=0, has_side_effects=True, vmem_limit_bytes=56 * 1024 * 1024
        ),
    )(features, weight, cotangent, cols, counts, tiles)
    return pl.pallas_call(
        finish,
        out_shape=tuple(jax.ShapeDtypeStruct(r.shape, r.dtype) for r in results),
        in_specs=[spec] * 3,
        out_specs=(spec,) * 3,
        compiler_params=pltpu.CompilerParams(vmem_limit_bytes=63 * 1024 * 1024),
    )(*results)


def solution(mesh):
    return jax.shard_map(
        body,
        mesh=mesh,
        in_specs=(
            P(("section", "rep"), None),
            P(),
            P(("section", "rep"), None),
            P("section", "rep", None, None, None, None),
            P("section", "rep", None, None),
            P("section", "rep", None),
        ),
        out_specs=(P(("section", "rep"), None), P(("section", "rep"), None), P()),
        check_vma=False,
    )
```

time: 679 us -> 145 us (0.21); the launches traced: 669 us -> 143 us
  waiting for transfers between devices: 481 us -> 0 us
  Pallas kernels: 0 us -> 142 us
  blocking collectives: 131 us -> 0 us
  starting transfers between devices: 19.1 us -> 0 us
  between operations: 13.8 us -> 0.64 us
  matrix products: 11.4 us -> 0 us
  local copies, waits for them, and re-layouts: 7.73 us -> 0 us
    psum x1 -> x0, waiting for transfers between devices: 262 us -> none  [body(): lax.psum(local_terms, ('section', 'rep')) / math.sqrt(total_nodes)]
    all_gather x2 -> x0, waiting for transfers between devices: 149 us -> none  [the longest x1 81.6 us: body(): lax.all_gather(grad_aggr, 'section', axis=0, tiled=True)]
    pallas_call x0 -> x2, Pallas kernels: none -> 142 us  [the longest x1 140 us: body(): pl.pallas_call(kernel, out_shape=(jax.ShapeDtypeStruct((TILE, D), BF16),...]
    all_to_all x2 -> x0, blocking collectives: 131 us -> none  [the longest x1 118 us: body(): lax.all_to_all(partials, 'section', split_axis=0, concat_axis=0, tiled=True)]
    reduce_scatter x1 -> x0, waiting for transfers between devices: 61.1 us -> none  [body(): lax.psum_scatter(terms.reshape(tile * lax.axis_size('rep'), width).astype...]
    all_to_all x2 -> x0, starting transfers between devices: 18.9 us -> none  [the longest x1 14.4 us: body(): lax.all_to_all(tile_counts, 'section', split_axis=2, concat_axis=0, tiled...]
    dot_general x6 -> x0, matrix products: 11.4 us -> none  [the longest x1 3.51 us: body(): jnp.einsum('tskj,tkd->tsjd', moved_masked, row_grads, preferred_element_t...]
    all_to_all x2 -> x0, waiting for transfers between devices: 8.51 us -> none  [the longest x1 8.51 us: body(): lax.all_to_all(tile_counts, 'section', split_axis=2, concat_axis=0, tiled...]
  transfers between devices with their start and end apart: 6 -> 0, of which waited for: 5 -> 0; matrix products, arithmetic and copies ran while one was open for 2% -> 0% of each run, Pallas kernels for 0% -> 0%
where the time goes in v1:
time: 145 us; the launch traced here: 143 us
  Pallas kernels  142 us (98%)
    pallas_call x1, Pallas kernels, body(): pl.pallas_call(kernel, out_shape=(jax.ShapeDtypeStruct((TILE, D), BF16),...  140 us

profile of v1, /device:TPU:1, one launch (start us, length us, event | category | flops | bytes accessed | tf_op | source)
XLA Modules:
  0.0 142.8 jit_solution(10416426490216252120)
XLA Ops:
  0.6 140.3 %shard_map.85 = (bf16[128,256]{1,0:T(8,128)(2,1)}, bf16[128,256]{1,0:T(8,128)(2,1)}, f32[256,256]{1,0:T(8,128)}) custom-call(bf16[128,256]{1,0:T(8,128)(2,1)} %feat_ref.1, bf16[256,256]{1,0:T(8,128)(2,1)} %weight_ref.1, bf16[128,256]{1,0:T(8,128)(2,1)} %cot_ref.1, s32[2,32]{1,0:T(2,128)} %bitcast.6, s32[1,32]{1,0:T(1,128)} %bitcast.7, ...), custom_call_target="tpu_custom_call" | custom-call | tf_op jit(solution)/shard_map/pallas_call | solution.py:420
  141.0 1.8 %shard_map.86 = (bf16[128,256]{1,0:T(8,128)(2,1)}, bf16[128,256]{1,0:T(8,128)(2,1)}, f32[256,256]{1,0:T(8,128)}) custom-call(bf16[128,256]{1,0:T(8,128)(2,1)} %get-tuple-element.6.out_in, bf16[128,256]{1,0:T(8,128)(2,1)} %get-tuple-element.7.gf_in, f32[256,256]{1,0:T(8,128)} %get-tuple-element.8.gw_in), custom_call_target="tpu_custom_call" | custom-call | tf_op jit(solution)/shard_map/pallas_call | solution.py:476

commit v2 on v1

v2 whole, which is shorter than its diff:
```python
import jax
import jax.numpy as jnp
from jax import lax
from jax.experimental import pallas as pl
from jax.experimental.pallas import tpu as pltpu
from jax.sharding import PartitionSpec as P

MESH = pl.DeviceIdType.MESH
F32 = jnp.float32
BF16 = jnp.bfloat16
NX, NY, NZ = 4, 8, 8
ZH = NZ // 2
GROUP = 2 * NX
SLOTS = 2
TILE = 128
D = 256
TERMS = ZH * GROUP * SLOTS
ZERO = TERMS


def device(x, y, z, k):
    return ((x // 2) * (2 * NZ) + z * 2 + k, y * 2 + x % 2)


def kernel(
    feat_ref, weight_ref, cot_ref, cols_ref, counts_ref, tiles_ref,
    out_ref, gf_ref, gw_ref,
    tiles_rx, meta_tx, meta_rx, meta_sm, prev_sm, last_sm,
    feats, part_tx, part_rx, grad_tx, grad_rx, chain,
    sib_tx, sib_rx, plus_tx, plus_rx, minus_tx, minus_rx, zred_tx, zred_rx,
    gw1_tx, gw1_rx, gw2_tx, gw2_rx, gw3_rx, gw4_rx, gw5_rx,
    local_sem, tile_s, tile_r, meta_s, meta_r, agz_s, agz_r,
    agp_s, agp_r, agm_s, agm_r, agd_s, agd_r, part_s, part_r, grad_s, grad_r,
    sib_s, sib_r, plus_s, plus_r, minus_s, minus_r, zred_s, zred_r,
    gw_s, gw_r,
):
    section, rep = lax.axis_index("section"), lax.axis_index("rep")
    xh, z, k = section // (2 * NZ), (section // 2) % NZ, section % 2
    y, xl = rep // 2, rep % 2
    x = 2 * xh + xl
    zp, zh = z % 2, z // 2
    member = x * 2 + k
    turn = 1 - 2 * k
    zpair = (z + turn * (1 - 2 * zp) + NZ) % NZ
    mine = x * 2 + zp
    sibling = device(x, y, z, 1 - k)

    def partner(j):
        return device(2 * xh + k, y, j * 2 + zp, xl)

    def yp(j):
        return (y + turn * j + 2 * NY) % NY

    def group(o):
        h = o // 2
        px, pz = (x + h + (h // 2) * (1 - 2 * (h % 2))) % NX, (zp + o % 2) % 2
        return px, pz, px * 2 + pz

    def peer(o):
        px, pz, p = group(o)
        return px, pz, p, device(px, y, zpair if o % 2 else z, k)

    def copy(src, dst, send, recv, dev):
        return pltpu.make_async_remote_copy(
            src_ref=src, dst_ref=dst, send_sem=send, recv_sem=recv,
            device_id=dev, device_id_type=MESH,
        )

    sent = []

    def send(src, dst, ssem, rsem, dev):
        c = copy(src, dst, ssem, rsem, dev)
        c.start()
        sent.append(c)

    def arrived(dst, ssem, rsem):
        copy(dst, dst, ssem, rsem, sibling).wait_recv()

    ypeers = [(y + i) % NY for i in range(1, NY)]
    zpeers = [(z + i) % NZ for i in range(1, NZ)]
    mpeers = [(member + i) % GROUP for i in range(1, GROUP)]

    own_tiles = pltpu.make_async_copy(
        tiles_ref.at[x // 2, :, zp, x % 2], tiles_rx.at[mine], local_sem.at[0]
    )
    own_tiles.start()

    barrier = pltpu.get_barrier_semaphore()
    everyone = (
        [device(x, j, z, k) for j in ypeers]
        + [device(x, y, j, k) for j in zpeers]
        + [device(j // 2, y, z, j % 2) for j in mpeers]
        + [peer(o)[3] for o in (3, 5, 7)]
        + [partner((zh + i) % ZH) for i in range(1, ZH)]
    )
    for dev in everyone:
        pl.semaphore_signal(barrier, inc=1, device_id=dev, device_id_type=MESH)
    pl.semaphore_wait(barrier, len(everyone))

    @pl.when(xl == k)
    def _():
        feats[k, y, zh] = feat_ref[...]

    @pl.when(xl != k)
    def _():
        copy(feat_ref, feats.at[xl, y, zh], agz_s.at[0], agz_r.at[zh], partner(zh)).start()

    zothers = [(zh + i) % ZH for i in range(ZH)]
    for i in range(1, ZH):
        send(feat_ref, feats.at[xl, y, zh], agz_s.at[i], agz_r.at[zh], partner(zothers[i]))

    dead = lax.broadcasted_iota(jnp.int32, (SLOTS, 32), 0) >= counts_ref[...]
    meta_tx[...] = jnp.zeros_like(meta_tx)
    meta_tx[0:SLOTS, 0:32] = cols_ref[...] + jnp.where(dead, 2 * NY, 0)
    for o in range(1, GROUP):
        px, pz, p, dev = peer(o)
        send(meta_tx, meta_rx.at[mine], meta_s.at[o], meta_r.at[mine], dev)
    meta_rx[mine] = meta_tx[...]

    def send_tiles(c):
        for o in range(1, GROUP):
            px, pz, p, dev = peer(o)
            send(
                tiles_ref.at[px // 2, c, pz, px % 2], tiles_rx.at[mine, c],
                tile_s.at[o, c], tile_r.at[mine, c], dev,
            )

    up, down = device(x, yp(1), z, k), device(x, yp(-1), z, k)

    def gather_plus(s, i):
        c, j = yp(-s), zothers[i]
        send(feats.at[k, c, j], feats.at[k, c, j], agp_s.at[s, i], agp_r.at[s, i], up)

    def gather_minus(s, i):
        c, j = yp(s), zothers[i]
        send(feats.at[k, c, j], feats.at[k, c, j], agm_s.at[s, i], agm_r.at[s, i], down)

    def gather_sibling(j):
        c = yp(j)
        send(feats.at[k, c], feats.at[k, c], agd_s.at[j % NY], agd_r.at[c], sibling)

    send_tiles(0)
    for i in range(ZH):
        j = zothers[i]
        if i == 0:
            @pl.when(xl != k)
            def _():
                arrived(feats.at[k, y, zh], agz_s.at[0], agz_r.at[zh])
        else:
            arrived(feats.at[k, y, j], agz_s.at[i], agz_r.at[j])
        gather_plus(0, i)
        gather_minus(0, i)
    gather_sibling(0)
    send_tiles(1)
    for s in range(4):
        for i in range(ZH):
            arrived(feats.at[k, yp(-s - 1), zothers[i]], agp_s.at[s, i], agp_r.at[s, i])
            if s < 3:
                gather_plus(s + 1, i)
                arrived(feats.at[k, yp(s + 1), zothers[i]], agm_s.at[s, i], agm_r.at[s, i])
                if s < 2:
                    gather_minus(s + 1, i)
        gather_sibling(-s - 1)
        if s < 3:
            gather_sibling(s + 1)
        if s < 2:
            send_tiles(s + 2)

    for o in range(1, GROUP):
        p = peer(o)[2]
        arrived(meta_rx.at[p], meta_s.at[o], meta_r.at[p])
    to_scalar = pltpu.make_async_copy(meta_rx, meta_sm, local_sem.at[1])
    to_scalar.start()
    to_scalar.wait()

    def column_section(c):
        return (x // 2) * (2 * NZ) + c * 4 + zp * 2 + x % 2

    @pl.loop(0, ZH * 2 * NY)
    def _(q):
        last_sm[q] = ZERO

    @pl.loop(0, TERMS)
    def _(i):
        c, o, s = i // (GROUP * SLOTS), (i // SLOTS) % GROUP, i % SLOTS
        col = meta_sm[group(o)[2], s, column_section(c)] % (2 * NY)
        prev_sm[i] = last_sm[c * 2 * NY + col]
        for q in range(2 * NY):
            last_sm[c * 2 * NY + q] = jnp.where(col == q, i, last_sm[c * 2 * NY + q])

    chain[ZERO] = jnp.zeros((D, TILE), F32)

    for j in range(NY):
        c = (y + j) % NY
        arrived(feats.at[1 - k, c], agd_s.at[0], agd_r.at[c])

    def live_tiles(p, c):
        tiles, codes = [], []
        for s in range(SLOTS):
            code = meta_sm[p, s, column_section(c)]
            tile = tiles_rx[p, c, s]
            tiles.append(jnp.where(code < 2 * NY, tile, jnp.zeros_like(tile)))
            codes.append(code % (2 * NY))
        return jnp.concatenate(tiles, axis=1), codes

    total = None
    for o in (1, 2, 3, 4, 5, 6, 7, 0):
        px, pz, p, dev = peer(o)
        if o == 0:
            own_tiles.wait()
        else:
            for c in range(ZH):
                arrived(tiles_rx.at[p, c], tile_s.at[o, c], tile_r.at[p, c])
        acc = jnp.zeros((TILE, D), F32)
        for c in range(ZH):
            pair, cols = live_tiles(p, c)
            rows = jnp.concatenate([feats[col % 2, col // 2, c] for col in cols], axis=0)
            acc += jnp.dot(pair, rows, preferred_element_type=F32)
        if o == 0:
            total = acc
        else:
            part_tx[o] = acc.astype(BF16)
            send(part_tx.at[o], part_rx.at[mine], part_s.at[o], part_r.at[mine], dev)
    for o in range(1, GROUP):
        p = peer(o)[2]
        arrived(part_rx.at[p], part_s.at[o], part_r.at[p])
        total += part_rx[p].astype(F32)

    aggregated = total.astype(BF16)
    weight = weight_ref[...]
    pre = jnp.dot(aggregated, weight, preferred_element_type=F32)
    sig = lax.logistic(pre)
    out_ref[...] = (pre * sig).astype(BF16)
    grad_pre = (cot_ref[...].astype(F32) * sig * (1.0 + pre * (1.0 - sig))).astype(BF16)
    grad_tx[...] = lax.dot_general(
        weight, grad_pre, (((1,), (1,)), ((), ())), preferred_element_type=F32
    ).astype(BF16)
    for o in range(1, GROUP):
        px, pz, p, dev = peer(o)
        send(grad_tx, grad_rx.at[mine], grad_s.at[o], grad_r.at[mine], dev)

    terms = lax.dot_general(
        aggregated, grad_pre, (((0,), (0,)), ((), ())), preferred_element_type=F32
    )
    for i in range(NZ):
        for j in range(GROUP):
            r0, c0 = i * 32 + (j % 4) * 8, (j // 4) * 128
            gw1_tx[i, j] = terms[r0:r0 + 8, c0:c0 + 128]
    for i, j in enumerate(zpeers):
        send(gw1_tx.at[j], gw1_rx.at[z], gw_s.at[0, i], gw_r.at[0, z], device(x, y, j, k))
    gw1_rx[z] = gw1_tx[z]

    for o in range(GROUP):
        px, pz, p, dev = peer(o)
        if o == 0:
            grads = grad_tx[...]
        else:
            arrived(grad_rx.at[p], grad_s.at[o], grad_r.at[p])
            grads = grad_rx[p]
        for c in range(ZH):
            pair, cols = live_tiles(p, c)
            both = jnp.dot(grads, pair, preferred_element_type=F32)
            for s in range(SLOTS):
                i = c * GROUP * SLOTS + o * SLOTS + s
                chain[i] = both[:, s * TILE:(s + 1) * TILE] + chain[prev_sm[i]]

    def block(c, yy, half):
        return chain[last_sm[c * 2 * NY + yy * 2 + half]]

    def send_half(j):
        yy = yp(j)
        for c in range(ZH):
            sib_tx[yy, c] = block(c, yy, 1 - k).astype(BF16)
        send(sib_tx.at[yy], sib_rx.at[yy], sib_s.at[j % NY], sib_r.at[yy], sibling)

    def both_cores(yy, c):
        return block(c, yy, k) + sib_rx[yy, c].astype(F32)

    def reduce_step(s, target, tx, rx, ssem, rsem, dev):
        arrived(sib_rx.at[target], sib_s.at[0], sib_r.at[target])
        for c in range(ZH):
            value = both_cores(target, c)
            if s > 0:
                arrived(rx.at[s - 1, c], ssem.at[s - 1, c], rsem.at[s - 1, c])
                value += rx[s - 1, c].astype(F32)
            tx[s, c] = value.astype(BF16)
            send(tx.at[s, c], rx.at[s, c], ssem.at[s, c], rsem.at[s, c], dev)

    def weight_round(s):
        if s == 0:
            for i, j in enumerate(zpeers):
                arrived(gw1_rx.at[j], gw_s.at[0, i], gw_r.at[0, j])
            gw2_tx[...] = jnp.sum(gw1_rx[...], axis=0)
            for i, j in enumerate(mpeers):
                send(gw2_tx.at[j], gw2_rx.at[member], gw_s.at[1, i], gw_r.at[1, member], device(j // 2, y, z, j % 2))
            gw2_rx[member] = gw2_tx[member]
        elif s == 1:
            for i, j in enumerate(mpeers):
                arrived(gw2_rx.at[j], gw_s.at[1, i], gw_r.at[1, j])
            gw3_rx[y] = jnp.sum(gw2_rx[...], axis=0)
            for i, j in enumerate(ypeers):
                send(gw3_rx.at[y], gw3_rx.at[y], gw_s.at[2, i], gw_r.at[2, y], device(x, j, z, k))
        elif s == 2:
            for i, j in enumerate(ypeers):
                arrived(gw3_rx.at[j], gw_s.at[2, i], gw_r.at[2, j])
            gw4_rx[member] = jnp.sum(gw3_rx[...], axis=0)
            for i, j in enumerate(mpeers):
                send(gw4_rx.at[member], gw4_rx.at[member], gw_s.at[3, i], gw_r.at[3, member], device(j // 2, y, z, j % 2))
        else:
            for i, j in enumerate(mpeers):
                arrived(gw4_rx.at[j], gw_s.at[3, i], gw_r.at[3, j])
            gw5_rx[z] = gw4_rx[...]
            for i, j in enumerate(zpeers):
                send(gw5_rx.at[z], gw5_rx.at[z], gw_s.at[4, i], gw_r.at[4, z], device(x, y, j, k))

    for s, halves in enumerate(((4, 3), (-3, 2), (-2, 1), (-1, 0))):
        for j in halves:
            send_half(j)
        reduce_step(s, yp(4 - s), plus_tx, plus_rx, plus_s, plus_r, up)
        if s < 3:
            reduce_step(s, yp(s - 3), minus_tx, minus_rx, minus_s, minus_r, down)
        weight_round(s)

    arrived(sib_rx.at[y], sib_s.at[0], sib_r.at[y])
    for c in range(ZH):
        arrived(plus_rx.at[3, c], plus_s.at[3, c], plus_r.at[3, c])
        arrived(minus_rx.at[2, c], minus_s.at[2, c], minus_r.at[2, c])
    for i in (1, 2, 3, 0):
        j = zothers[i]
        value = both_cores(y, j) + plus_rx[3, j].astype(F32) + minus_rx[2, j].astype(F32)
        zred_tx[i] = value.astype(BF16)
        if i > 0:
            send(zred_tx.at[i], zred_rx.at[zh], zred_s.at[i], zred_r.at[zh], partner(j))

    @pl.when(xl == k)
    def _():
        zred_rx[zh] = zred_tx[0]

    @pl.when(xl != k)
    def _():
        copy(zred_tx.at[0], zred_rx.at[zh], zred_s.at[0], zred_r.at[zh], partner(zh)).start()

    for i, j in enumerate(zpeers):
        arrived(gw5_rx.at[j], gw_s.at[4, i], gw_r.at[4, j])
    scale = 1.0 / 256.0
    for i in range(NZ):
        for j in range(GROUP):
            r0, c0 = i * 32 + (j % 4) * 8, (j // 4) * 128
            gw_ref[r0:r0 + 8, c0:c0 + 128] = gw5_rx[i, j] * scale

    for i in range(1, ZH):
        arrived(zred_rx.at[zothers[i]], zred_s.at[i], zred_r.at[zothers[i]])

    @pl.when(xl != k)
    def _():
        arrived(zred_rx.at[zh], zred_s.at[0], zred_r.at[zh])

    gf_ref[...] = jnp.sum(zred_rx[...].astype(F32), axis=0).T.astype(BF16)

    @pl.when(xl != k)
    def _():
        copy(zred_tx.at[0], zred_rx.at[zh], zred_s.at[0], zred_r.at[zh], partner(zh)).wait_send()
        copy(feat_ref, feats.at[xl, y, zh], agz_s.at[0], agz_r.at[zh], partner(zh)).wait_send()

    for c in sent:
        c.wait_send()


def finish(out_in, gf_in, gw_in, out_ref, gf_ref, gw_ref):
    out_ref[...] = out_in[...]
    gf_ref[...] = gf_in[...]
    gw_ref[...] = gw_in[...]


def body(features, weight, cotangent, tile_values, tile_cols, tile_counts):
    cols = tile_cols.reshape(32, SLOTS).T
    counts = tile_counts.reshape(1, 32)
    tiles = tile_values.reshape(2, ZH, 2, 2, SLOTS, TILE, TILE)
    dma, vmem = pltpu.SemaphoreType.DMA, pltpu.VMEM
    spec = pl.BlockSpec(memory_space=pltpu.VMEM)
    block = (D, TILE)
    results = pl.pallas_call(
        kernel,
        out_shape=(
            jax.ShapeDtypeStruct((TILE, D), BF16),
            jax.ShapeDtypeStruct((TILE, D), BF16),
            jax.ShapeDtypeStruct((D, D), F32),
        ),
        in_specs=[spec] * 5 + [pl.BlockSpec(memory_space=pl.ANY)],
        out_specs=(spec,) * 3,
        scratch_shapes=[
            vmem((GROUP, ZH, SLOTS, TILE, TILE), BF16),
            vmem((8, 128), jnp.int32),
            vmem((GROUP, 8, 128), jnp.int32),
            pltpu.SMEM((GROUP, 8, 128), jnp.int32),
            pltpu.SMEM((TERMS,), jnp.int32),
            pltpu.SMEM((ZH * 2 * NY,), jnp.int32),
            vmem((2, NY, ZH, TILE, D), BF16),
            vmem((GROUP, TILE, D), BF16),
            vmem((GROUP, TILE, D), BF16),
            vmem(block, BF16),
            vmem((GROUP,) + block, BF16),
            vmem((TERMS + 1,) + block, F32),
            vmem((NY, ZH) + block, BF16),
            vmem((NY, ZH) + block, BF16),
            vmem((4, ZH) + block, BF16),
            vmem((4, ZH) + block, BF16),
            vmem((3, ZH) + block, BF16),
            vmem((3, ZH) + block, BF16),
            vmem((ZH,) + block, BF16),
            vmem((ZH,) + block, BF16),
            vmem((NZ, GROUP, 8, 128), F32),
            vmem((NZ, GROUP, 8, 128), F32),
            vmem((GROUP, 8, 128), F32),
            vmem((GROUP, 8, 128), F32),
            vmem((NY, 8, 128), F32),
            vmem((GROUP, 8, 128), F32),
            vmem((NZ, GROUP, 8, 128), F32),
            dma((2,)),
            dma((GROUP, ZH)), dma((GROUP, ZH)),
            dma((GROUP,)), dma((GROUP,)),
            dma((ZH,)), dma((ZH,)),
            dma((4, ZH)), dma((4, ZH)),
            dma((3, ZH)), dma((3, ZH)),
            dma((NY,)), dma((NY,)),
            dma((GROUP,)), dma((GROUP,)),
            dma((GROUP,)), dma((GROUP,)),
            dma((NY,)), dma((NY,)),
            dma((4, ZH)), dma((4, ZH)),
            dma((3, ZH)), dma((3, ZH)),
            dma((ZH,)), dma((ZH,)),
            dma((5, 8)), dma((5, 8)),
        ],
        compiler_params=pltpu.CompilerParams(
            collective_id=0, has_side_effects=True, vmem_limit_bytes=56 * 1024 * 1024
        ),
    )(features, weight, cotangent, cols, counts, tiles)
    return pl.pallas_call(
        finish,
        out_shape=tuple(jax.ShapeDtypeStruct(r.shape, r.dtype) for r in results),
        in_specs=[spec] * 3,
        out_specs=(spec,) * 3,
        compiler_params=pltpu.CompilerParams(vmem_limit_bytes=63 * 1024 * 1024),
    )(*results)


def solution(mesh):
    return jax.shard_map(
        body,
        mesh=mesh,
        in_specs=(
            P(("section", "rep"), None),
            P(),
            P(("section", "rep"), None),
            P("section", "rep", None, None, None, None),
            P("section", "rep", None, None),
            P("section", "rep", None),
        ),
        out_specs=(P(("section", "rep"), None), P(("section", "rep"), None), P()),
        check_vma=False,
    )
```

time: 145 us -> 115 us (0.79); the launches traced: 143 us -> 114 us
  Pallas kernels: 142 us -> 114 us
    pallas_call x1, Pallas kernels: 140 us -> 112 us  [body(): pl.pallas_call(kernel, out_shape=(jax.ShapeDtypeStruct((TILE, D), BF16),...]
where the time goes in v2:
time: 115 us; the launch traced here: 114 us
  Pallas kernels  114 us (99%)
    pallas_call x1, Pallas kernels, body(): pl.pallas_call(kernel, out_shape=(jax.ShapeDtypeStruct((TILE, D), BF16),...  112 us

profile of v2, /device:TPU:1, one launch (start us, length us, event | category | flops | bytes accessed | tf_op | source)
XLA Modules:
  0.0 114.5 jit_solution(10124194089445957018)
XLA Ops:
  0.6 112.0 %shard_map.85 = (bf16[128,256]{1,0:T(8,128)(2,1)}, bf16[128,256]{1,0:T(8,128)(2,1)}, f32[256,256]{1,0:T(8,128)}) custom-call(bf16[128,256]{1,0:T(8,128)(2,1)} %feat_ref.1, bf16[256,256]{1,0:T(8,128)(2,1)} %weight_ref.1, bf16[128,256]{1,0:T(8,128)(2,1)} %cot_ref.1, s32[2,32]{1,0:T(2,128)} %bitcast.6, s32[1,32]{1,0:T(1,128)} %bitcast.7, ...), custom_call_target="tpu_custom_call" | custom-call | tf_op jit(solution)/shard_map/pallas_call | solution.py:382
  112.7 1.8 %shard_map.86 = (bf16[128,256]{1,0:T(8,128)(2,1)}, bf16[128,256]{1,0:T(8,128)(2,1)}, f32[256,256]{1,0:T(8,128)}) custom-call(bf16[128,256]{1,0:T(8,128)(2,1)} %get-tuple-element.6.out_in, bf16[128,256]{1,0:T(8,128)(2,1)} %get-tuple-element.7.gf_in, f32[256,256]{1,0:T(8,128)} %get-tuple-element.8.gw_in), custom_call_target="tpu_custom_call" | custom-call | tf_op jit(solution)/shard_map/pallas_call | solution.py:438

commit v3 on v2

--- a/solution.py
+++ b/solution.py
@@ -15,6 +15,7 @@
 TILE = 128
 D = 256
 TERMS = ZH * GROUP * SLOTS
+ORDER = (0, 4, 2, 1, 6, 5, 3, 7)
 ZERO = TERMS
 
 
@@ -26,10 +27,10 @@
     feat_ref, weight_ref, cot_ref, cols_ref, counts_ref, tiles_ref,
     out_ref, gf_ref, gw_ref,
     tiles_rx, meta_tx, meta_rx, meta_sm, prev_sm, last_sm,
-    feats, part_tx, part_rx, grad_tx, grad_rx, chain,
+    feats, relay_rx, part_tx, part_pass, part_rx, grad_tx, grad_rx, chain,
     sib_tx, sib_rx, plus_tx, plus_rx, minus_tx, minus_rx, zred_tx, zred_rx,
     gw1_tx, gw1_rx, gw2_tx, gw2_rx, gw3_rx, gw4_rx, gw5_rx,
-    local_sem, tile_s, tile_r, meta_s, meta_r, agz_s, agz_r,
+    local_sem, relay_s, relay_r, pass_r, tile_s, tile_r, meta_s, meta_r, agz_s, agz_r,
     agp_s, agp_r, agm_s, agm_r, agd_s, agd_r, part_s, part_r, grad_s, grad_r,
     sib_s, sib_r, plus_s, plus_r, minus_s, minus_r, zred_s, zred_r,
     gw_s, gw_r,
@@ -53,7 +54,8 @@
 
     def group(o):
         h = o // 2
-        px, pz = (x + h + (h // 2) * (1 - 2 * (h % 2))) % NX, (zp + o % 2) % 2
+        px = (x + turn * (h + (h // 2) * (1 - 2 * (h % 2))) + 2 * NX) % NX
+        pz = (zp + o % 2) % 2
         return px, pz, px * 2 + pz
 
     def peer(o):
@@ -118,12 +120,19 @@
     meta_rx[mine] = meta_tx[...]
 
     def send_tiles(c):
-        for o in range(1, GROUP):
+        for o in (6, 7, 2, 3, 4, 5, 1):
             px, pz, p, dev = peer(o)
-            send(
-                tiles_ref.at[px // 2, c, pz, px % 2], tiles_rx.at[mine, c],
-                tile_s.at[o, c], tile_r.at[mine, c], dev,
-            )
+            dst, rsem = tiles_rx.at[mine, c], tile_r.at[mine, c]
+            if o >= 6:
+                dst, rsem, dev = relay_rx.at[o - 6, c], relay_r.at[o - 6, c], peer(2)[3]
+            send(tiles_ref.at[px // 2, c, pz, px % 2], dst, tile_s.at[o, c], rsem, dev)
+
+    before = group(4)[2]
+
+    def pass_tiles(c):
+        for o in range(2):
+            arrived(relay_rx.at[o, c], relay_s.at[o, c], relay_r.at[o, c])
+            send(relay_rx.at[o, c], tiles_rx.at[before, c], relay_s.at[o, c], tile_r.at[before, c], peer(2 + o)[3])
 
     up, down = device(x, yp(1), z, k), device(x, yp(-1), z, k)
 
@@ -165,6 +174,7 @@
             gather_sibling(s + 1)
         if s < 2:
             send_tiles(s + 2)
+        pass_tiles(s)
 
     for o in range(1, GROUP):
         p = peer(o)[2]
@@ -180,13 +190,17 @@
     def _(q):
         last_sm[q] = ZERO
 
-    @pl.loop(0, TERMS)
-    def _(i):
-        c, o, s = i // (GROUP * SLOTS), (i // SLOTS) % GROUP, i % SLOTS
-        col = meta_sm[group(o)[2], s, column_section(c)] % (2 * NY)
-        prev_sm[i] = last_sm[c * 2 * NY + col]
-        for q in range(2 * NY):
-            last_sm[c * 2 * NY + q] = jnp.where(col == q, i, last_sm[c * 2 * NY + q])
+    for n, o in enumerate(ORDER):
+        p = group(o)[2]
+
+        @pl.loop(0, ZH * SLOTS)
+        def _(t):
+            c, s = t // SLOTS, t % SLOTS
+            i = c * (GROUP * SLOTS) + n * SLOTS + s
+            col = meta_sm[p, s, column_section(c)] % (2 * NY)
+            prev_sm[i] = last_sm[c * 2 * NY + col]
+            for q in range(2 * NY):
+                last_sm[c * 2 * NY + q] = jnp.where(col == q, i, last_sm[c * 2 * NY + q])
 
     chain[ZERO] = jnp.zeros((D, TILE), F32)
 
@@ -204,7 +218,7 @@
         return jnp.concatenate(tiles, axis=1), codes
 
     total = None
-    for o in (1, 2, 3, 4, 5, 6, 7, 0):
+    for o in (6, 7, 4, 5, 1, 2, 3, 0):
         px, pz, p, dev = peer(o)
         if o == 0:
             own_tiles.wait()
@@ -219,9 +233,15 @@
         if o == 0:
             total = acc
         else:
+            if o in (2, 3):
+                arrived(part_pass.at[o - 2], part_s.at[o], pass_r.at[o - 2])
+                acc += part_pass[o - 2].astype(F32)
             part_tx[o] = acc.astype(BF16)
-            send(part_tx.at[o], part_rx.at[mine], part_s.at[o], part_r.at[mine], dev)
-    for o in range(1, GROUP):
+            dst, rsem = part_rx.at[mine], part_r.at[mine]
+            if o >= 6:
+                dst, rsem, dev = part_pass.at[o - 6], pass_r.at[o - 6], peer(2)[3]
+            send(part_tx.at[o], dst, part_s.at[o], rsem, dev)
+    for o in range(1, 6):
         p = peer(o)[2]
         arrived(part_rx.at[p], part_s.at[o], part_r.at[p])
         total += part_rx[p].astype(F32)
@@ -235,9 +255,14 @@
     grad_tx[...] = lax.dot_general(
         weight, grad_pre, (((1,), (1,)), ((), ())), preferred_element_type=F32
     ).astype(BF16)
-    for o in range(1, GROUP):
-        px, pz, p, dev = peer(o)
-        send(grad_tx, grad_rx.at[mine], grad_s.at[o], grad_r.at[mine], dev)
+    for n, o in enumerate((4, 2, 1)):
+        send(grad_tx, grad_rx.at[mine], grad_s.at[n], grad_r.at[mine], peer(o)[3])
+
+    def pass_grads(o, n, targets):
+        p = group(o)[2]
+        arrived(grad_rx.at[p], grad_s.at[n], grad_r.at[p])
+        for i, t in enumerate(targets):
+            send(grad_rx.at[p], grad_rx.at[p], grad_s.at[n + i], grad_r.at[p], peer(t)[3])
 
     terms = lax.dot_general(
         aggregated, grad_pre, (((0,), (0,)), ((), ())), preferred_element_type=F32
@@ -250,18 +275,21 @@
         send(gw1_tx.at[j], gw1_rx.at[z], gw_s.at[0, i], gw_r.at[0, z], device(x, y, j, k))
     gw1_rx[z] = gw1_tx[z]
 
-    for o in range(GROUP):
-        px, pz, p, dev = peer(o)
-        if o == 0:
-            grads = grad_tx[...]
-        else:
-            arrived(grad_rx.at[p], grad_s.at[o], grad_r.at[p])
-            grads = grad_rx[p]
+    for n, o in enumerate(ORDER):
+        p = group(o)[2]
+        if n == 1:
+            pass_grads(4, 3, (2, 1))
+            pass_grads(2, 5, (1,))
+        elif n == 4:
+            pass_grads(6, 6, (1,))
+        elif o in (1, 5, 3, 7):
+            arrived(grad_rx.at[p], grad_s.at[0], grad_r.at[p])
+        grads = grad_rx[p] if o else grad_tx[...]
         for c in range(ZH):
             pair, cols = live_tiles(p, c)
             both = jnp.dot(grads, pair, preferred_element_type=F32)
             for s in range(SLOTS):
-                i = c * GROUP * SLOTS + o * SLOTS + s
+                i = c * GROUP * SLOTS + n * SLOTS + s
                 chain[i] = both[:, s * TILE:(s + 1) * TILE] + chain[prev_sm[i]]
 
     def block(c, yy, half):
@@ -396,7 +424,9 @@
             pltpu.SMEM((TERMS,), jnp.int32),
             pltpu.SMEM((ZH * 2 * NY,), jnp.int32),
             vmem((2, NY, ZH, TILE, D), BF16),
+            vmem((2, ZH, SLOTS, TILE, TILE), BF16),
             vmem((GROUP, TILE, D), BF16),
+            vmem((2, TILE, D), BF16),
             vmem((GROUP, TILE, D), BF16),
             vmem(block, BF16),
             vmem((GROUP,) + block, BF16),
@@ -417,6 +447,7 @@
             vmem((GROUP, 8, 128), F32),
             vmem((NZ, GROUP, 8, 128), F32),
             dma((2,)),
+            dma((2, ZH)), dma((2, ZH)), dma((2,)),
             dma((GROUP, ZH)), dma((GROUP, ZH)),
             dma((GROUP,)), dma((GROUP,)),
             dma((ZH,)), dma((ZH,)),

time: 115 us -> 115 us (level)
  no operation moved by 1% of the time
where the time goes in v3:
time: 115 us; the launch traced here: 114 us
  Pallas kernels  114 us (99%)
    pallas_call x1, Pallas kernels, body(): pl.pallas_call(kernel, out_shape=(jax.ShapeDtypeStruct((TILE, D), BF16),...  112 us

profile of v3, /device:TPU:1, one launch (start us, length us, event | category | flops | bytes accessed | tf_op | source)
XLA Modules:
  0.0 114.3 jit_solution(225961667425350330)
XLA Ops:
  0.6 111.9 %shard_map.85 = (bf16[128,256]{1,0:T(8,128)(2,1)}, bf16[128,256]{1,0:T(8,128)(2,1)}, f32[256,256]{1,0:T(8,128)}) custom-call(bf16[128,256]{1,0:T(8,128)(2,1)} %feat_ref.1, bf16[256,256]{1,0:T(8,128)(2,1)} %weight_ref.1, bf16[128,256]{1,0:T(8,128)(2,1)} %cot_ref.1, s32[2,32]{1,0:T(2,128)} %bitcast.6, s32[1,32]{1,0:T(1,128)} %bitcast.7, ...), custom_call_target="tpu_custom_call" | custom-call | tf_op jit(solution)/shard_map/pallas_call | solution.py:410
  112.5 1.8 %shard_map.86 = (bf16[128,256]{1,0:T(8,128)(2,1)}, bf16[128,256]{1,0:T(8,128)(2,1)}, f32[256,256]{1,0:T(8,128)}) custom-call(bf16[128,256]{1,0:T(8,128)(2,1)} %get-tuple-element.6.out_in, bf16[128,256]{1,0:T(8,128)(2,1)} %get-tuple-element.7.gf_in, f32[256,256]{1,0:T(8,128)} %get-tuple-element.8.gw_in), custom_call_target="tpu_custom_call" | custom-call | tf_op jit(solution)/shard_map/pallas_call | solution.py:469

commit v4 on v2

--- a/solution.py
+++ b/solution.py
@@ -125,6 +125,31 @@
                 tile_s.at[o, c], tile_r.at[mine, c], dev,
             )
 
+    def column_section(c):
+        return (x // 2) * (2 * NZ) + c * 4 + zp * 2 + x % 2
+
+    def column_table():
+        for o in range(1, GROUP):
+            p = peer(o)[2]
+            arrived(meta_rx.at[p], meta_s.at[o], meta_r.at[p])
+        to_scalar = pltpu.make_async_copy(meta_rx, meta_sm, local_sem.at[1])
+        to_scalar.start()
+        to_scalar.wait()
+
+        @pl.loop(0, ZH * 2 * NY)
+        def _(q):
+            last_sm[q] = ZERO
+
+        @pl.loop(0, TERMS)
+        def _(i):
+            c, o, s = i // (GROUP * SLOTS), (i // SLOTS) % GROUP, i % SLOTS
+            col = meta_sm[group(o)[2], s, column_section(c)] % (2 * NY)
+            prev_sm[i] = last_sm[c * 2 * NY + col]
+            for q in range(2 * NY):
+                last_sm[c * 2 * NY + q] = jnp.where(col == q, i, last_sm[c * 2 * NY + q])
+
+        chain[ZERO] = jnp.zeros((D, TILE), F32)
+
     up, down = device(x, yp(1), z, k), device(x, yp(-1), z, k)
 
     def gather_plus(s, i):
@@ -153,6 +178,8 @@
     gather_sibling(0)
     send_tiles(1)
     for s in range(4):
+        if s == 3:
+            column_table()
         for i in range(ZH):
             arrived(feats.at[k, yp(-s - 1), zothers[i]], agp_s.at[s, i], agp_r.at[s, i])
             if s < 3:
@@ -165,30 +192,6 @@
             gather_sibling(s + 1)
         if s < 2:
             send_tiles(s + 2)
-
-    for o in range(1, GROUP):
-        p = peer(o)[2]
-        arrived(meta_rx.at[p], meta_s.at[o], meta_r.at[p])
-    to_scalar = pltpu.make_async_copy(meta_rx, meta_sm, local_sem.at[1])
-    to_scalar.start()
-    to_scalar.wait()
-
-    def column_section(c):
-        return (x // 2) * (2 * NZ) + c * 4 + zp * 2 + x % 2
-
-    @pl.loop(0, ZH * 2 * NY)
-    def _(q):
-        last_sm[q] = ZERO
-
-    @pl.loop(0, TERMS)
-    def _(i):
-        c, o, s = i // (GROUP * SLOTS), (i // SLOTS) % GROUP, i % SLOTS
-        col = meta_sm[group(o)[2], s, column_section(c)] % (2 * NY)
-        prev_sm[i] = last_sm[c * 2 * NY + col]
-        for q in range(2 * NY):
-            last_sm[c * 2 * NY + q] = jnp.where(col == q, i, last_sm[c * 2 * NY + q])
-
-    chain[ZERO] = jnp.zeros((D, TILE), F32)
 
     for j in range(NY):
         c = (y + j) % NY
@@ -249,42 +252,6 @@
     for i, j in enumerate(zpeers):
         send(gw1_tx.at[j], gw1_rx.at[z], gw_s.at[0, i], gw_r.at[0, z], device(x, y, j, k))
     gw1_rx[z] = gw1_tx[z]
-
-    for o in range(GROUP):
-        px, pz, p, dev = peer(o)
-        if o == 0:
-            grads = grad_tx[...]
-        else:
-            arrived(grad_rx.at[p], grad_s.at[o], grad_r.at[p])
-            grads = grad_rx[p]
-        for c in range(ZH):
-            pair, cols = live_tiles(p, c)
-            both = jnp.dot(grads, pair, preferred_element_type=F32)
-            for s in range(SLOTS):
-                i = c * GROUP * SLOTS + o * SLOTS + s
-                chain[i] = both[:, s * TILE:(s + 1) * TILE] + chain[prev_sm[i]]
-
-    def block(c, yy, half):
-        return chain[last_sm[c * 2 * NY + yy * 2 + half]]
-
-    def send_half(j):
-        yy = yp(j)
-        for c in range(ZH):
-            sib_tx[yy, c] = block(c, yy, 1 - k).astype(BF16)
-        send(sib_tx.at[yy], sib_rx.at[yy], sib_s.at[j % NY], sib_r.at[yy], sibling)
-
-    def both_cores(yy, c):
-        return block(c, yy, k) + sib_rx[yy, c].astype(F32)
-
-    def reduce_step(s, target, tx, rx, ssem, rsem, dev):
-        arrived(sib_rx.at[target], sib_s.at[0], sib_r.at[target])
-        for c in range(ZH):
-            value = both_cores(target, c)
-            if s > 0:
-                arrived(rx.at[s - 1, c], ssem.at[s - 1, c], rsem.at[s - 1, c])
-                value += rx[s - 1, c].astype(F32)
-            tx[s, c] = value.astype(BF16)
-            send(tx.at[s, c], rx.at[s, c], ssem.at[s, c], rsem.at[s, c], dev)
 
     def weight_round(s):
         if s == 0:
@@ -313,20 +280,58 @@
             for i, j in enumerate(zpeers):
                 send(gw5_rx.at[z], gw5_rx.at[z], gw_s.at[4, i], gw_r.at[4, z], device(x, y, j, k))
 
+    for o in range(GROUP):
+        px, pz, p, dev = peer(o)
+        if o == 0:
+            grads = grad_tx[...]
+        else:
+            arrived(grad_rx.at[p], grad_s.at[o], grad_r.at[p])
+            grads = grad_rx[p]
+        for c in range(ZH):
+            pair, cols = live_tiles(p, c)
+            both = jnp.dot(grads, pair, preferred_element_type=F32)
+            for s in range(SLOTS):
+                i = c * GROUP * SLOTS + o * SLOTS + s
+                chain[i] = both[:, s * TILE:(s + 1) * TILE] + chain[prev_sm[i]]
+        if o in (4, 6):
+            weight_round(o // 2 - 2)
+
+    def block(c, yy, half):
+        return chain[last_sm[c * 2 * NY + yy * 2 + half]]
+
+    def send_half(j):
+        yy = yp(j)
+        for c in range(ZH):
+            sib_tx[yy, c] = block(c, yy, 1 - k).astype(BF16)
+        send(sib_tx.at[yy], sib_rx.at[yy], sib_s.at[j % NY], sib_r.at[yy], sibling)
+
+    def both_cores(yy, c):
+        return block(c, yy, k) + sib_rx[yy, c].astype(F32)
+
+    def reduce_step(s, target, tx, rx, ssem, rsem, dev):
+        arrived(sib_rx.at[target], sib_s.at[0], sib_r.at[target])
+        for c in (zothers[2], zothers[1], zothers[3], zh):
+            value = both_cores(target, c)
+            if s > 0:
+                arrived(rx.at[s - 1, c], ssem.at[s - 1, c], rsem.at[s - 1, c])
+                value += rx[s - 1, c].astype(F32)
+            tx[s, c] = value.astype(BF16)
+            send(tx.at[s, c], rx.at[s, c], ssem.at[s, c], rsem.at[s, c], dev)
+
     for s, halves in enumerate(((4, 3), (-3, 2), (-2, 1), (-1, 0))):
         for j in halves:
             send_half(j)
         reduce_step(s, yp(4 - s), plus_tx, plus_rx, plus_s, plus_r, up)
         if s < 3:
             reduce_step(s, yp(s - 3), minus_tx, minus_rx, minus_s, minus_r, down)
-        weight_round(s)
+        if s < 2:
+            weight_round(s + 2)
 
     arrived(sib_rx.at[y], sib_s.at[0], sib_r.at[y])
-    for c in range(ZH):
-        arrived(plus_rx.at[3, c], plus_s.at[3, c], plus_r.at[3, c])
-        arrived(minus_rx.at[2, c], minus_s.at[2, c], minus_r.at[2, c])
-    for i in (1, 2, 3, 0):
+    for i in (2, 1, 3, 0):
         j = zothers[i]
+        arrived(plus_rx.at[3, j], plus_s.at[3, j], plus_r.at[3, j])
+        arrived(minus_rx.at[2, j], minus_s.at[2, j], minus_r.at[2, j])
         value = both_cores(y, j) + plus_rx[3, j].astype(F32) + minus_rx[2, j].astype(F32)
         zred_tx[i] = value.astype(BF16)
         if i > 0:

time: 115 us -> 113 us (0.983)
  no operation moved by 1% of the time
where the time goes in v4:
time: 113 us
  Pallas kernels  113 us (100%)
    pallas_call x1, Pallas kernels, body(): pl.pallas_call(kernel, out_shape=(jax.ShapeDtypeStruct((TILE, D), BF16),...  111 us

profile of v4, /device:TPU:1, one launch (start us, length us, event | category | flops | bytes accessed | tf_op | source)
XLA Modules:
  0.0 113.3 jit_solution(17408731865814532034)
XLA Ops:
  0.6 110.9 %shard_map.85 = (bf16[128,256]{1,0:T(8,128)(2,1)}, bf16[128,256]{1,0:T(8,128)(2,1)}, f32[256,256]{1,0:T(8,128)}) custom-call(bf16[128,256]{1,0:T(8,128)(2,1)} %feat_ref.1, bf16[256,256]{1,0:T(8,128)(2,1)} %weight_ref.1, bf16[128,256]{1,0:T(8,128)(2,1)} %cot_ref.1, s32[2,32]{1,0:T(2,128)} %bitcast.6, s32[1,32]{1,0:T(1,128)} %bitcast.7, ...), custom_call_target="tpu_custom_call" | custom-call | tf_op jit(solution)/shard_map/pallas_call | solution.py:387
  111.5 1.8 %shard_map.86 = (bf16[128,256]{1,0:T(8,128)(2,1)}, bf16[128,256]{1,0:T(8,128)(2,1)}, f32[256,256]{1,0:T(8,128)}) custom-call(bf16[128,256]{1,0:T(8,128)(2,1)} %get-tuple-element.6.out_in, bf16[128,256]{1,0:T(8,128)(2,1)} %get-tuple-element.7.gf_in, f32[256,256]{1,0:T(8,128)} %get-tuple-element.8.gw_in), custom_call_target="tpu_custom_call" | custom-call | tf_op jit(solution)/shard_map/pallas_call | solution.py:443

commit v5 on v4

--- a/solution.py
+++ b/solution.py
@@ -15,6 +15,7 @@
 TILE = 128
 D = 256
 TERMS = ZH * GROUP * SLOTS
+ORDER = (0, 4, 2, 1, 6, 5, 3, 7)
 ZERO = TERMS
 
 
@@ -26,10 +27,10 @@
     feat_ref, weight_ref, cot_ref, cols_ref, counts_ref, tiles_ref,
     out_ref, gf_ref, gw_ref,
     tiles_rx, meta_tx, meta_rx, meta_sm, prev_sm, last_sm,
-    feats, part_tx, part_rx, grad_tx, grad_rx, chain,
+    feats, part_tx, part_pass, part_rx, grad_tx, grad_rx, chain,
     sib_tx, sib_rx, plus_tx, plus_rx, minus_tx, minus_rx, zred_tx, zred_rx,
     gw1_tx, gw1_rx, gw2_tx, gw2_rx, gw3_rx, gw4_rx, gw5_rx,
-    local_sem, tile_s, tile_r, meta_s, meta_r, agz_s, agz_r,
+    local_sem, pass_r, tile_s, tile_r, meta_s, meta_r, agz_s, agz_r,
     agp_s, agp_r, agm_s, agm_r, agd_s, agd_r, part_s, part_r, grad_s, grad_r,
     sib_s, sib_r, plus_s, plus_r, minus_s, minus_r, zred_s, zred_r,
     gw_s, gw_r,
@@ -53,7 +54,8 @@
 
     def group(o):
         h = o // 2
-        px, pz = (x + h + (h // 2) * (1 - 2 * (h % 2))) % NX, (zp + o % 2) % 2
+        px = (x + turn * (h + (h // 2) * (1 - 2 * (h % 2))) + 2 * NX) % NX
+        pz = (zp + o % 2) % 2
         return px, pz, px * 2 + pz
 
     def peer(o):
@@ -140,13 +142,17 @@
         def _(q):
             last_sm[q] = ZERO
 
-        @pl.loop(0, TERMS)
-        def _(i):
-            c, o, s = i // (GROUP * SLOTS), (i // SLOTS) % GROUP, i % SLOTS
-            col = meta_sm[group(o)[2], s, column_section(c)] % (2 * NY)
-            prev_sm[i] = last_sm[c * 2 * NY + col]
-            for q in range(2 * NY):
-                last_sm[c * 2 * NY + q] = jnp.where(col == q, i, last_sm[c * 2 * NY + q])
+        for n, o in enumerate(ORDER):
+            p = group(o)[2]
+
+            @pl.loop(0, ZH * SLOTS)
+            def _(t):
+                c, s = t // SLOTS, t % SLOTS
+                i = c * (GROUP * SLOTS) + n * SLOTS + s
+                col = meta_sm[p, s, column_section(c)] % (2 * NY)
+                prev_sm[i] = last_sm[c * 2 * NY + col]
+                for q in range(2 * NY):
+                    last_sm[c * 2 * NY + q] = jnp.where(col == q, i, last_sm[c * 2 * NY + q])
 
         chain[ZERO] = jnp.zeros((D, TILE), F32)
 
@@ -207,7 +213,7 @@
         return jnp.concatenate(tiles, axis=1), codes
 
     total = None
-    for o in (1, 2, 3, 4, 5, 6, 7, 0):
+    for o in (6, 7, 4, 5, 1, 2, 3, 0):
         px, pz, p, dev = peer(o)
         if o == 0:
             own_tiles.wait()
@@ -222,9 +228,15 @@
         if o == 0:
             total = acc
         else:
+            if o in (2, 3):
+                arrived(part_pass.at[o - 2], part_s.at[o], pass_r.at[o - 2])
+                acc += part_pass[o - 2].astype(F32)
             part_tx[o] = acc.astype(BF16)
-            send(part_tx.at[o], part_rx.at[mine], part_s.at[o], part_r.at[mine], dev)
-    for o in range(1, GROUP):
+            dst, rsem = part_rx.at[mine], part_r.at[mine]
+            if o >= 6:
+                dst, rsem, dev = part_pass.at[o - 6], pass_r.at[o - 6], peer(2)[3]
+            send(part_tx.at[o], dst, part_s.at[o], rsem, dev)
+    for o in range(1, 6):
         p = peer(o)[2]
         arrived(part_rx.at[p], part_s.at[o], part_r.at[p])
         total += part_rx[p].astype(F32)
@@ -238,9 +250,14 @@
     grad_tx[...] = lax.dot_general(
         weight, grad_pre, (((1,), (1,)), ((), ())), preferred_element_type=F32
     ).astype(BF16)
-    for o in range(1, GROUP):
-        px, pz, p, dev = peer(o)
-        send(grad_tx, grad_rx.at[mine], grad_s.at[o], grad_r.at[mine], dev)
+    for n, o in enumerate((4, 2, 1)):
+        send(grad_tx, grad_rx.at[mine], grad_s.at[n], grad_r.at[mine], peer(o)[3])
+
+    def pass_grads(o, n, targets):
+        p = group(o)[2]
+        arrived(grad_rx.at[p], grad_s.at[n], grad_r.at[p])
+        for i, t in enumerate(targets):
+            send(grad_rx.at[p], grad_rx.at[p], grad_s.at[n + i], grad_r.at[p], peer(t)[3])
 
     terms = lax.dot_general(
         aggregated, grad_pre, (((0,), (0,)), ((), ())), preferred_element_type=F32
@@ -280,21 +297,25 @@
             for i, j in enumerate(zpeers):
                 send(gw5_rx.at[z], gw5_rx.at[z], gw_s.at[4, i], gw_r.at[4, z], device(x, y, j, k))
 
-    for o in range(GROUP):
-        px, pz, p, dev = peer(o)
-        if o == 0:
-            grads = grad_tx[...]
-        else:
-            arrived(grad_rx.at[p], grad_s.at[o], grad_r.at[p])
-            grads = grad_rx[p]
+    for n, o in enumerate(ORDER):
+        p = group(o)[2]
+        if n == 1:
+            pass_grads(4, 3, (2, 1))
+            pass_grads(2, 5, (1,))
+        elif n == 3:
+            pass_grads(6, 6, (1,))
+            arrived(grad_rx.at[p], grad_s.at[0], grad_r.at[p])
+        elif o in (5, 3, 7):
+            arrived(grad_rx.at[p], grad_s.at[0], grad_r.at[p])
+        grads = grad_rx[p] if o else grad_tx[...]
         for c in range(ZH):
             pair, cols = live_tiles(p, c)
             both = jnp.dot(grads, pair, preferred_element_type=F32)
             for s in range(SLOTS):
-                i = c * GROUP * SLOTS + o * SLOTS + s
+                i = c * GROUP * SLOTS + n * SLOTS + s
                 chain[i] = both[:, s * TILE:(s + 1) * TILE] + chain[prev_sm[i]]
-        if o in (4, 6):
-            weight_round(o // 2 - 2)
+        if n in (3, 5):
+            weight_round((n - 3) // 2)
 
     def block(c, yy, half):
         return chain[last_sm[c * 2 * NY + yy * 2 + half]]
@@ -402,6 +423,7 @@
             pltpu.SMEM((ZH * 2 * NY,), jnp.int32),
             vmem((2, NY, ZH, TILE, D), BF16),
             vmem((GROUP, TILE, D), BF16),
+            vmem((2, TILE, D), BF16),
             vmem((GROUP, TILE, D), BF16),
             vmem(block, BF16),
             vmem((GROUP,) + block, BF16),
@@ -421,7 +443,7 @@
             vmem((NY, 8, 128), F32),
             vmem((GROUP, 8, 128), F32),
             vmem((NZ, GROUP, 8, 128), F32),
-            dma((2,)),
+            dma((2,)), dma((2,)),
             dma((GROUP, ZH)), dma((GROUP, ZH)),
             dma((GROUP,)), dma((GROUP,)),
             dma((ZH,)), dma((ZH,)),

time: 113 us -> 111 us (0.982)
  Pallas kernels: 113 us -> 110 us
    pallas_call x1, Pallas kernels: 111 us -> 108 us  [body(): pl.pallas_call(kernel, out_shape=(jax.ShapeDtypeStruct((TILE, D), BF16),...]
where the time goes in v5:
time: 111 us
  Pallas kernels  110 us (99%)
    pallas_call x1, Pallas kernels, body(): pl.pallas_call(kernel, out_shape=(jax.ShapeDtypeStruct((TILE, D), BF16),...  108 us

profile of v5, /device:TPU:1, one launch (start us, length us, event | category | flops | bytes accessed | tf_op | source)
XLA Modules:
  0.0 110.6 jit_solution(11630858859385827731)
XLA Ops:
  0.6 108.2 %shard_map.85 = (bf16[128,256]{1,0:T(8,128)(2,1)}, bf16[128,256]{1,0:T(8,128)(2,1)}, f32[256,256]{1,0:T(8,128)}) custom-call(bf16[128,256]{1,0:T(8,128)(2,1)} %feat_ref.1, bf16[256,256]{1,0:T(8,128)(2,1)} %weight_ref.1, bf16[128,256]{1,0:T(8,128)(2,1)} %cot_ref.1, s32[2,32]{1,0:T(2,128)} %bitcast.6, s32[1,32]{1,0:T(1,128)} %bitcast.7, ...), custom_call_target="tpu_custom_call" | custom-call | tf_op jit(solution)/shard_map/pallas_call | solution.py:408
  108.8 1.8 %shard_map.86 = (bf16[128,256]{1,0:T(8,128)(2,1)}, bf16[128,256]{1,0:T(8,128)(2,1)}, f32[256,256]{1,0:T(8,128)}) custom-call(bf16[128,256]{1,0:T(8,128)(2,1)} %get-tuple-element.6.out_in, bf16[128,256]{1,0:T(8,128)(2,1)} %get-tuple-element.7.gf_in, f32[256,256]{1,0:T(8,128)} %get-tuple-element.8.gw_in), custom_call_target="tpu_custom_call" | custom-call | tf_op jit(solution)/shard_map/pallas_call | solution.py:465

commit v6 on v5

--- a/solution.py
+++ b/solution.py
@@ -120,7 +120,7 @@
     meta_rx[mine] = meta_tx[...]
 
     def send_tiles(c):
-        for o in range(1, GROUP):
+        for o in (6, 7, 4, 5, 1, 2, 3):
             px, pz, p, dev = peer(o)
             send(
                 tiles_ref.at[px // 2, c, pz, px % 2], tiles_rx.at[mine, c],

time: 111 us -> 111 us (level)
  no operation moved by 1% of the time
where the time goes in v6:
time: 111 us
  Pallas kernels  110 us (99%)
    pallas_call x1, Pallas kernels, body(): pl.pallas_call(kernel, out_shape=(jax.ShapeDtypeStruct((TILE, D), BF16),...  108 us

profile of v6, /device:TPU:1, one launch (start us, length us, event | category | flops | bytes accessed | tf_op | source)
XLA Modules:
  0.0 110.5 jit_solution(9567502416433951798)
XLA Ops:
  0.6 108.1 %shard_map.85 = (bf16[128,256]{1,0:T(8,128)(2,1)}, bf16[128,256]{1,0:T(8,128)(2,1)}, f32[256,256]{1,0:T(8,128)}) custom-call(bf16[128,256]{1,0:T(8,128)(2,1)} %feat_ref.1, bf16[256,256]{1,0:T(8,128)(2,1)} %weight_ref.1, bf16[128,256]{1,0:T(8,128)(2,1)} %cot_ref.1, s32[2,32]{1,0:T(2,128)} %bitcast.6, s32[1,32]{1,0:T(1,128)} %bitcast.7, ...), custom_call_target="tpu_custom_call" | custom-call | tf_op jit(solution)/shard_map/pallas_call | solution.py:408
  108.8 1.8 %shard_map.86 = (bf16[128,256]{1,0:T(8,128)(2,1)}, bf16[128,256]{1,0:T(8,128)(2,1)}, f32[256,256]{1,0:T(8,128)}) custom-call(bf16[128,256]{1,0:T(8,128)(2,1)} %get-tuple-element.6.out_in, bf16[128,256]{1,0:T(8,128)(2,1)} %get-tuple-element.7.gf_in, f32[256,256]{1,0:T(8,128)} %get-tuple-element.8.gw_in), custom_call_target="tpu_custom_call" | custom-call | tf_op jit(solution)/shard_map/pallas_call | solution.py:465
